TPU v7x, 32 devices: a whole 2x2x4 slice. The times are simulated.
32 devices in a mesh: grp: 2 (over x), mk: 8 (over z, y), tile: 2 (over core).
Axes of the slice: x: 2, y: 2, z: 4, core: 2. Of those that a mesh axis runs over, the one named last changes fastest.
Arguments:
- dosage: bfloat16 [3072, 16384], P(('grp', 'tile'), 'mk'), parts along dimension 0, may hold values from 0 to 2
- allele_freq: float32 [32768], P(('grp', 'mk')), parts along dimension 0, may hold values from 0.05 to 0.5
- present: int32 [256, 3072], P('mk', ('grp', 'tile')), parts along dimension 1, may hold values 0 or 1
- panel_rows: int32 [32], P('grp'), parts along dimension 0, may hold values from 1 to 192, 1536 in all
Outputs:
- panels: float32 [6144, 1536], P(('grp', 'mk', 'tile')), parts along dimension 0
There are 2 independent parts, one for each index of `grp`. A program takes and returns all parts, laid end to end along the dimension named above; each array names one. Nothing has to cross between parts.
Inputs may be any that keep to these rules, and one draw needn't show every extreme that they name: `panel_rows`: the counts sum to 1536.
All inputs are finite; a program needn't handle non-finite values. No bound on the sum of `present` on one device may be relied on, other than what follows from the above.
Results may differ from a plain program's by a relative error of at most 0.0011.
Values may be sent and summed in bfloat16 or wider, within the bound.
A program may use at most 64 MiB of HBM per device.

v0:
```python
import jax
import jax.numpy as jnp
from jax import lax
from jax.sharding import PartitionSpec as P


def local(dosage, allele_freq, present, panel_rows):
    tile_count = lax.axis_size("tile")
    local_markers = dosage.shape[1]
    marker_total = local_markers * lax.axis_size("mk")
    flags = jnp.repeat(present.T, local_markers // present.shape[0], axis=1).astype(jnp.float32)
    twice_freq = 2.0 * allele_freq
    scaled = (dosage.astype(jnp.float32) - twice_freq) / jnp.sqrt(twice_freq * (1.0 - allele_freq))
    standard = (flags * scaled).astype(jnp.bfloat16)
    all_rows = lax.all_gather(standard, "tile", axis=0, tiled=True)
    samples = all_rows.shape[0]
    owner_count = lax.axis_size("mk") * tile_count
    panel_max = 2 * samples // owner_count
    starts = jnp.cumsum(panel_rows) - panel_rows
    row_ids = jnp.arange(panel_max * tile_count * lax.axis_size("mk"), dtype=jnp.int32)
    owner_ids = row_ids // panel_max
    within = row_ids - owner_ids * panel_max
    sample_ids = jnp.take(starts, owner_ids) + within
    live = within < jnp.take(panel_rows, owner_ids)
    picked = jnp.take(all_rows, jnp.clip(sample_ids, 0, samples - 1), axis=0)
    picked = jnp.where(live[:, None], picked, jnp.zeros((), jnp.bfloat16))
    product = jnp.einsum("rm,sm->rs", picked, standard, preferred_element_type=jnp.float32)
    pair_rows = lax.psum_scatter(
        product * (1.0 / marker_total), "mk", scatter_dimension=0, tiled=True
    )
    return lax.all_to_all(pair_rows, "tile", split_axis=0, concat_axis=1, tiled=True)


def solution(mesh):
    in_specs = (P(("grp", "tile"), "mk"), P(("grp", "mk")), P("mk", ("grp", "tile")), P("grp"))
    out_specs = P(("grp", "mk", "tile"), None)
    return jax.shard_map(local, mesh=mesh, in_specs=in_specs, out_specs=out_specs, check_vma=False)
```

profile of v0, /device:TPU:1, one launch (start us, length us, event | category | flops | bytes accessed | tf_op | source)
XLA Modules:
  0.0 279.0 jit_solution(269421417285457136)
XLA Ops:
  6.5 0.0 all-gather.2.cloned.1.call-start
  6.5 0.7 broadcast_multiply_fusion
  7.2 0.9 convert_bitcast_fusion
  8.1 3.1 %broadcast_in_dim.38 = f32[768,32,64]{0,2,1:T(8,128)} broadcast(f32[768,32]{0,1:T(8,128)S(1)} %convert_bitcast_fusion), dimensions={0,1} | broadcast | bytes 6389760 | tf_op jit(solution)/shard_map/broadcast_in_dim | solution.py:11
  11.3 0.0 copy-start.1
  11.3 6.7 %copy.9 = f32[768,2048]{1,0:T(8,128)} copy(f32[768,2048]{0,1:T(8,128)} %bitcast.41) | data formatting | bytes 12582912 | tf_op jit(solution)/shard_map/convert_element_type | solution.py:11
  18.0 0.0 copy-done.1
  18.0 0.0 copy-start.2
  18.0 5.6 %multiply_convert_fusion = bf16[768,2048]{1,0:T(8,128)(2,1)} fusion(f32[768,2048]{1,0:T(8,128)} %copy.9, bf16[768,2048]{1,0:T(8,128)(2,1)S(1)} %copy-done.1, f32[2048]{0:T(1024)S(1)} %get-tuple-element.7, f32[2048]{0:T(1024)S(1)} %get-tuple-element.6), kind=kLoop, calls=%fused_computation.8 | loop fusion | flops 7864320 | bytes 12599296 | tf_op jit(solution)/shard_map/convert_element_type | solution.py:14
  23.6 0.0 all-gather.2.cloned.1.call-update
  23.7 0.0 reduce-scatter.2.cloned.1.call-start
  23.7 0.0 copy-done.2
  23.7 0.1 copy.8
  23.9 0.1 reduce
  24.0 0.7 fusion.17
  24.7 9.9 %compare_and_fusion.1 = pred[3072]{0:T(1024)(128)(4,1)S(1)} fusion(s32[]{:T(128)} %bitcast.32, s32[]{:T(128)} %bitcast.31, s32[]{:T(128)} %bitcast.30, s32[]{:T(128)} %bitcast.29, s32[]{:T(128)} %bitcast.28, s32[]{:T(128)} %bitcast.27, s32[]{:T(128)} %bitcast.26, s32[]{:T(128)} %bitcast.25, s32[]{:T(128)} %bitcast.24, s32[]{:T(128)} %bitcast.23, ...), kind=kLoop, calls=%fused_computation.25 | loop fusion | flops 168960 | bytes 3136 | tf_op jit(solution)/shard_map/jit(_take)/and | solution.py:25
  34.6 0.7 fusion.16
  35.3 10.2 %select_compare_fusion = pred[3072]{0:T(1024)(128)(4,1)S(1)} fusion(s32[]{:T(128)} %bitcast.15, s32[]{:T(128)} %bitcast.14, s32[]{:T(128)} %bitcast.13, s32[]{:T(128)} %bitcast.12, s32[]{:T(128)} %bitcast.11, s32[]{:T(128)} %bitcast.10, s32[]{:T(128)} %bitcast.9, s32[]{:T(128)} %bitcast.8, s32[]{:T(128)} %bitcast.7, s32[]{:T(128)} %bitcast.6, s32[]{:T(128)} %bitcast.5, ...), kind=kLoop, calls=%fused_computation.22 | loop fusion | flops 147456 | bytes 3136 | tf_op jit(solution)/shard_map/lt | solution.py:24
  45.5 9.9 %broadcast_clamp_fusion = s32[3072]{0:T(1024)S(1)} fusion(s32[]{:T(128)} %bitcast.32, s32[]{:T(128)} %bitcast.31, s32[]{:T(128)} %bitcast.30, s32[]{:T(128)} %bitcast.29, s32[]{:T(128)} %bitcast.28, s32[]{:T(128)} %bitcast.27, s32[]{:T(128)} %bitcast.26, s32[]{:T(128)} %bitcast.25, s32[]{:T(128)} %bitcast.24, s32[]{:T(128)} %bitcast.23, s32[]{:T(128)} %bitcast.22, ...), kind=kLoop, calls=%fused_computation.27 | loop fusion | flops 162816 | bytes 12352 | tf_op jit(solution)/shard_map/jit(_take)/gather | solution.py:25
  55.4 0.0 copy-start
  55.4 0.0 all-gather.2.cloned.1.call-done
  55.5 27.6 %gather_fusion = bf16[3072,2048]{1,0:T(8,128)(2,1)} fusion(bf16[1536,2048]{1,0:T(8,128)(2,1)} %all-gather.2.cloned.1.call-done, s32[3072]{0:T(1024)S(1)} %broadcast_clamp_fusion), kind=kCustom, calls=%fused_computation | custom fusion | bytes 25178112 | tf_op jit(solution)/shard_map/jit(_take)/gather | solution.py:25
  83.0 0.0 copy-done
  83.0 16.2 %fusion.7 = f32[3072,768]{1,0:T(8,128)} fusion(bf16[768,2048]{1,0:T(8,128)(2,1)S(1)} %copy-done, bf16[3072,2048]{1,0:T(8,128)(2,1)} %gather_fusion, pred[3072]{0:T(1024)(128)(4,1)S(1)} %compare_and_fusion.1, pred[3072]{0:T(1024)(128)(4,1)S(1)} %select_compare_fusion), kind=kOutput, calls=%fused_computation.9 | convolution fusion | flops 9678618624 | bytes 25171968 | tf_op jit(solution)/shard_map/rm,sm->rs/dot_general | solution.py:27
  99.2 0.0 reduce-scatter.2.cloned.1.call-update
  99.2 165.7 %reduce-scatter.2.cloned.1.call-done = f32[384,768]{1,0:T(8,128)} async-done(((f32[3072,768]{1,0:T(8,128)}), f32[384,768]{1,0:T(8,128)}) %reduce-scatter.2.cloned.1.call-update) | async-done | bytes 1179664 | tf_op jit(solution)/shard_map/reduce_scatter | solution.py:28
  264.9 6.0 %all_to_all.19 = f32[2,192,768]{2,1,0:T(8,128)S(1)} all-to-all(f32[2,192,768]{2,1,0:T(8,128)} %bitcast.43), channel_id=1, replica_groups=mesh['grp'=2,'mk'=8,'tile'=2] {'tile'}, dimensions={0} | all-to-all | bytes 2359296 | tf_op jit(solution)/shard_map/all_to_all | solution.py:31
  271.0 1.2 copy.11
  (2 shorter events, 0.0 us)
Async XLA Ops:
  6.5 48.9 %all-gather.2.cloned.1.call-start = ((), (), s32[]{:S(2)}) async-start(), calls=%async_computation.2 | async-start | bytes 9437184 | tf_op jit(solution)/shard_map/all_gather | solution.py:15
  11.3 6.7 %copy-start.1 = (bf16[768,2048]{1,0:T(8,128)(2,1)S(1)}, bf16[768,2048]{1,0:T(8,128)(2,1)}, u32[]{:S(2)}) copy-start(bf16[768,2048]{1,0:T(8,128)(2,1)} %param.6) | copy-start | bytes 9437188
  18.0 5.7 %copy-start.2 = (s32[16]{0:T(128)S(1)}, s32[16]{0:T(128)}, u32[]{:S(2)}) copy-start(s32[16]{0:T(128)} %param.9) | copy-start | bytes 196
  23.7 241.3 %reduce-scatter.2.cloned.1.call-start = ((), (), s32[]{:S(2)}) async-start(), calls=%async_computation.3 | async-start | bytes 10616832 | tf_op jit(solution)/shard_map/reduce_scatter | solution.py:28
  55.4 27.6 %copy-start = (bf16[768,2048]{1,0:T(8,128)(2,1)S(1)}, bf16[768,2048]{1,0:T(8,128)(2,1)}, u32[]{:S(2)}) copy-start(bf16[768,2048]{1,0:T(8,128)(2,1)} %multiply_convert_fusion) | copy-start | bytes 9437188
Sparse Core Ops, SparseCore 0:
  23.8 19.2 all-gather.1
  99.3 165.5 reduce-scatter.1
where the time goes:
time: 280 us; the launch traced here: 279 us
  waiting for transfers between devices  166 us (59%)
  local copies, waits for them, and re-layouts  40.1 us (14%)
  other arithmetic  37.4 us (13%)
  matrix products  16.2 us (6%)
  between operations  13.5 us (5%)
  blocking collectives  6.03 us (2%)
    reduce_scatter x1, waiting for transfers between devices, local(): lax.psum_scatter(product * (1.0 / marker_total), 'mk', scatter_dimension=...  166 us
    gather x1, local copies, waits for them, and re-layouts, local(): picked = jnp.take(all_rows, jnp.clip(sample_ids, 0, samples - 1), axis=0)  27.6 us
    dot_general x1, matrix products, local(): jnp.einsum('rm,sm->rs', picked, standard, preferred_element_type=jnp.floa...  16.2 us
    lt x1, other arithmetic, local(): live = within < jnp.take(panel_rows, owner_ids)  10.2 us
    and x1, other arithmetic, local(): picked = jnp.take(all_rows, jnp.clip(sample_ids, 0, samples - 1), axis=0)  9.9 us
    gather x1, other arithmetic, local(): picked = jnp.take(all_rows, jnp.clip(sample_ids, 0, samples - 1), axis=0)  9.88 us
    convert_element_type x1, local copies, waits for them, and re-layouts, local(): jnp.repeat(present.T, local_markers // present.shape[0], axis=1)  6.71 us
    all_to_all x1, blocking collectives, local(): lax.all_to_all(pair_rows, 'tile', split_axis=0, concat_axis=1, tiled=True)  6.03 us
  transfers between devices with their start and end apart: 2, of which 1 were waited for; matrix products, arithmetic and copies ran while one was open for 11% of the time, Pallas kernels for 0%

commit v1 on v0

--- a/solution.py
+++ b/solution.py
@@ -1,10 +1,259 @@
+import functools
+
 import jax
 import jax.numpy as jnp
 from jax import lax
+from jax.experimental import pallas as pl
+from jax.experimental.pallas import tpu as pltpu
 from jax.sharding import PartitionSpec as P
 
-
-def local(dosage, allele_freq, present, panel_rows):
+MESH = pl.DeviceIdType.MESH
+NT = (((1,), (1,)), ((), ()))
+TN = (((0,), (0,)), ((), ()))
+UP = 64.0
+
+
+def encode(x):
+    return (x * jnp.abs(x) * (x * x)).astype(jnp.bfloat16)
+
+
+def decode(v):
+    v = v.astype(jnp.float32)
+    root = lax.rsqrt(lax.rsqrt(jnp.abs(v)))
+    return jnp.where(v == 0.0, 0.0, jnp.where(v < 0.0, -root, root))
+
+
+def kernel(mk_y, mk_z, markers, dosage, freq, present, rows_ref, out, *scratch):
+    half, depth = dosage.shape
+    row_blk = half // 3
+    hy = row_blk // mk_y
+    sl = hy // mk_z
+    widths = [row_blk * (a + 1) for a in range(3)] + [half // 2] * 3
+    chunks = len(widths)
+    it = iter(scratch)
+    dos, std, hot = next(it), next(it), next(it)
+    ys, yr, zs, zr, acc, fin = ([next(it) for _ in range(chunks)] for _ in range(6))
+    (dos_sem, std_s, std_r, y_s, y_r, z_s, z_r, gz_s, gz_r, gy_s, gy_r, t_s, t_r) = it
+
+    mk, t = lax.axis_index("mk"), lax.axis_index("tile")
+    y, z = lax.rem(mk, mk_y), mk // mk_y
+    oy, ot = 1 - y, 1 - t
+
+    loads = [
+        pltpu.make_async_copy(
+            dosage.at[pl.ds(a * row_blk, row_blk)], dos.at[pl.ds(a * row_blk, row_blk)], dos_sem.at[a]
+        )
+        for a in range(3)
+    ]
+    for load in loads:
+        load.start()
+
+    to_y = {"mk": z * mk_y + oy}
+    to_t = {"tile": ot}
+
+    def to_z(k):
+        return {"mk": lax.rem(z + k, mk_z) * mk_y + y}
+
+    barrier = pltpu.get_barrier_semaphore()
+    peers = [to_y, to_t] + [to_z(k) for k in range(1, mk_z)]
+    for peer in peers:
+        pl.semaphore_signal(barrier, inc=1, device_id=peer, device_id_type=MESH)
+
+    owner = mk * 2 + t
+    start = jnp.int32(0)
+    count = jnp.int32(0)
+    for k in range(rows_ref.shape[0]):
+        here = rows_ref[k]
+        start = start + jnp.where(k < owner, here, 0)
+        count = count + jnp.where(k == owner, here, 0)
+    i_row = lax.broadcasted_iota(jnp.int32, hot.shape, 0)
+    i_col = lax.broadcasted_iota(jnp.int32, hot.shape, 1)
+    hot[...] = jnp.where((i_col - start == i_row) & (i_row < count), 1.0, 0.0).astype(jnp.bfloat16)
+    out[...] = jnp.zeros_like(out)
+
+    flag_blocks = present.shape[0]
+    per_flag = depth // flag_blocks
+    twice = 2.0 * freq[...]
+    scale = UP / jnp.sqrt(twice * (1.0 - freq[...]))
+    COL = 512
+
+    def standardize(a):
+        def piece(p, carry):
+            r0 = pl.multiple_of(a * row_blk + p * 128, 128)
+            called = present[:, pl.ds(r0, 128)].astype(jnp.float32).astype(jnp.bfloat16)
+            for c in range(depth // COL):
+                cols = slice(c * COL, (c + 1) * COL)
+                b = lax.broadcasted_iota(jnp.int32, (flag_blocks, COL), 0)
+                m = lax.broadcasted_iota(jnp.int32, (flag_blocks, COL), 1) + c * COL
+                spread = jnp.where((m >= b * per_flag) & (m < (b + 1) * per_flag), 1.0, 0.0).astype(jnp.bfloat16)
+                flags = lax.dot_general(called, spread, TN, preferred_element_type=jnp.float32)
+                scaled = (dos[pl.ds(r0, 128), cols].astype(jnp.float32) - twice[:, cols]) * scale[:, cols]
+                std[pl.ds(pl.multiple_of(t * half + r0, 128), 128), cols] = (flags * scaled).astype(jnp.bfloat16)
+            return carry
+
+        lax.fori_loop(0, row_blk // 128, piece, 0)
+
+    def place(c, core):
+        a = c % 3
+        if c < 3:
+            return core * half + a * row_blk, core * half
+        return a * row_blk, half + core * (half // 2)
+
+    def product(c, which):
+        i0, j0 = place(c, t)
+        left = std[pl.ds(pl.multiple_of(i0 + which * hy, 128), hy), :]
+        right = std[pl.ds(pl.multiple_of(j0, 128), widths[c]), :]
+        return lax.dot_general(left, right, NT, preferred_element_type=jnp.float32)
+
+    def remote(src, dst, send, recv, peer):
+        return pltpu.make_async_remote_copy(
+            src_ref=src, dst_ref=dst, send_sem=send, recv_sem=recv, device_id=peer, device_id_type=MESH
+        )
+
+    sent = []
+
+    def go(copy):
+        copy.start()
+        sent.append(copy)
+
+    def std_copy(a, core):
+        view = std.at[pl.ds(pl.multiple_of(core * half + a * row_blk, 128), row_blk)]
+        return remote(view, view, std_s.at[a], std_r.at[a], to_t)
+
+    def y_copy(c):
+        return remote(ys[c], yr[c], y_s.at[c], y_r.at[c], to_y)
+
+    def zrows(r):
+        return pl.ds(pl.multiple_of(r * sl, sl), sl)
+
+    def z_copy(c, k, source):
+        return remote(zs[c].at[zrows(lax.rem(z + k, mk_z))], zr[c].at[zrows(source)], z_s.at[c, k], z_r.at[c, k], to_z(k))
+
+    def gz_copy(c, k, source):
+        view = fin[c].at[t, pl.ds(pl.multiple_of(y * hy + source * sl, sl), sl)]
+        return remote(view, view, gz_s.at[c, k], gz_r.at[c, k], to_z(k))
+
+    def gy_copy(c, which):
+        view = fin[c].at[t, pl.ds(pl.multiple_of(which * hy, hy), hy)]
+        return remote(view, view, gy_s.at[c], gy_r.at[c], to_y)
+
+    def t_copy(c, step, core):
+        which = y if step == 0 else oy
+        view = fin[c].at[core, pl.ds(pl.multiple_of(which * hy, hy), hy)]
+        return remote(view, view, t_s.at[c, step], t_r.at[c, step], to_t)
+
+    def send_half(c):
+        ys[c][...] = encode(product(c, oy))
+        go(y_copy(c))
+
+    def own_half(c):
+        acc[c][...] = product(c, y)
+
+    def select(c, core):
+        i0, j0 = place(c, core)
+        w = widths[c]
+        block = fin[c][core]
+        rows = pl.ds(pl.multiple_of(i0, 128), row_blk)
+        cols = pl.ds(pl.multiple_of(j0, 128), w)
+        out[:, cols] += jnp.dot(hot[:, rows], block, preferred_element_type=jnp.float32)
+        below = w - row_blk if c < 3 else w
+        if below:
+            cols = pl.ds(pl.multiple_of(j0, 128), below)
+            out[:, rows] += lax.dot_general(
+                hot[:, cols], block[:, :below], NT, preferred_element_type=jnp.float32
+            )
+
+    for a in range(3):
+        loads[a].wait()
+        standardize(a)
+        if a == 0:
+            pl.semaphore_wait(barrier, len(peers))
+        go(std_copy(a, t))
+        send_half(a)
+    for a in range(3):
+        own_half(a)
+    for a in range(3):
+        std_copy(a, ot).wait_recv()
+    for a in range(3, 6):
+        send_half(a)
+    for a in range(3, 6):
+        own_half(a)
+
+    def stage_b(c):
+        y_copy(c).wait_recv()
+        total = acc[c][...] + decode(yr[c][...])
+        acc[c][...] = total
+        zs[c][...] = encode(total)
+        for k in range(1, mk_z):
+            go(z_copy(c, k, z))
+
+    def stage_c(c):
+        total = acc[c][zrows(z), :]
+        for k in range(1, mk_z):
+            source = lax.rem(z + mk_z - k, mk_z)
+            z_copy(c, k, source).wait_recv()
+            total = total + decode(zr[c][zrows(source), :])
+        fin[c][t, pl.ds(pl.multiple_of(y * hy + z * sl, sl), sl), :] = encode(total)
+        for k in range(1, mk_z):
+            go(gz_copy(c, k, z))
+
+    def stage_d(c):
+        for k in range(1, mk_z):
+            gz_copy(c, k, lax.rem(z + mk_z - k, mk_z)).wait_recv()
+        go(gy_copy(c, y))
+        go(t_copy(c, 0, t))
+
+    def stage_e(c):
+        gy_copy(c, oy).wait_recv()
+        go(t_copy(c, 1, t))
+        select(c, t)
+
+    def stage_f(c):
+        t_copy(c, 0, ot).wait_recv()
+        t_copy(c, 1, ot).wait_recv()
+        select(c, ot)
+
+    stages = [stage_b, stage_c, stage_d, stage_e, stage_f]
+    for s in range(chunks + len(stages) - 1):
+        for d, stage in enumerate(stages):
+            if 0 <= s - d < chunks:
+                stage(s - d)
+    for r in range(0, out.shape[0], 32):
+        out[r : r + 32, :] = decode(out[r : r + 32, :]) * (1.0 / (markers * UP * UP))
+    for copy in sent:
+        copy.wait_send()
+
+
+def fused(mesh, dosage, allele_freq, present, panel_rows):
+    mk_y, mk_z = 2, mesh.shape["mk"] // 2
+    half, depth = dosage.shape
+    samples = 2 * half
+    panel_max = 2 * samples // (2 * mesh.shape["mk"])
+    row_blk = half // 3
+    widths = [row_blk * (a + 1) for a in range(3)] + [half // 2] * 3
+    hy = row_blk // 2
+    bf, f32 = jnp.bfloat16, jnp.float32
+    scratch = [pltpu.VMEM((half, depth), bf), pltpu.VMEM((samples, depth), bf), pltpu.VMEM((panel_max, samples), bf)]
+    for dtype in (bf, bf, bf, bf, f32):
+        scratch += [pltpu.VMEM((hy, w), dtype) for w in widths]
+    scratch += [pltpu.VMEM((2, row_blk, w), bf) for w in widths]
+    n = len(widths)
+    for shape in [(3,)] * 3 + [(n,)] * 2 + [(n, mk_z)] * 4 + [(n,)] * 2 + [(n, 2)] * 2:
+        scratch.append(pltpu.SemaphoreType.DMA(shape))
+    vmem = pl.BlockSpec(memory_space=pltpu.VMEM)
+    return pl.pallas_call(
+        functools.partial(kernel, mk_y, mk_z, depth * mesh.shape["mk"]),
+        out_shape=jax.ShapeDtypeStruct((panel_max, samples), f32),
+        in_specs=[pl.BlockSpec(memory_space=pl.ANY), vmem, vmem, pl.BlockSpec(memory_space=pltpu.SMEM)],
+        out_specs=vmem,
+        scratch_shapes=scratch,
+        compiler_params=pltpu.CompilerParams(
+            collective_id=0, has_side_effects=True, vmem_limit_bytes=44 * 1024 * 1024
+        ),
+    )(dosage, allele_freq.reshape(1, depth), present, panel_rows)
+
+
+def general(dosage, allele_freq, present, panel_rows):
     tile_count = lax.axis_size("tile")
     local_markers = dosage.shape[1]
     marker_total = local_markers * lax.axis_size("mk")
@@ -16,7 +265,8 @@
     samples = all_rows.shape[0]
     owner_count = lax.axis_size("mk") * tile_count
     panel_max = 2 * samples // owner_count
-    starts = jnp.cumsum(panel_rows) - panel_rows
+    order = jnp.arange(owner_count)
+    starts = jnp.sum(jnp.where(order[None, :] < order[:, None], panel_rows[None, :], 0), axis=1)
     row_ids = jnp.arange(panel_max * tile_count * lax.axis_size("mk"), dtype=jnp.int32)
     owner_ids = row_ids // panel_max
     within = row_ids - owner_ids * panel_max
@@ -34,4 +284,5 @@
 def solution(mesh):
     in_specs = (P(("grp", "tile"), "mk"), P(("grp", "mk")), P("mk", ("grp", "tile")), P("grp"))
     out_specs = P(("grp", "mk", "tile"), None)
+    local = functools.partial(fused, mesh) if mesh.shape["mk"] == 8 else general
     return jax.shard_map(local, mesh=mesh, in_specs=in_specs, out_specs=out_specs, check_vma=False)

time: 280 us -> 62.1 us (0.22)
  waiting for transfers between devices: 166 us -> 0 us
  Pallas kernels: 0 us -> 56.7 us
  other arithmetic: 37.4 us -> 0 us
  local copies, waits for them, and re-layouts: 40.1 us -> 5.15 us
  matrix products: 16.2 us -> 0 us
  between operations: 13.5 us -> 0.01 us
  blocking collectives: 6.03 us -> 0 us
    reduce_scatter x1 -> x0, waiting for transfers between devices: 166 us -> none  [local(): lax.psum_scatter(product * (1.0 / marker_total), 'mk', scatter_dimension=...]
    pallas_call x0 -> x1, Pallas kernels: none -> 56.7 us  [fused(): pl.pallas_call(functools.partial(kernel, mk_y, mk_z, depth * mesh.shape['...]
    gather x3 -> x0, local copies, waits for them, and re-layouts: 29 us -> none  [the longest x1 27.6 us: local(): picked = jnp.take(all_rows, jnp.clip(sample_ids, 0, samples - 1), axis=0)]
    dot_general x1 -> x0, matrix products: 16.2 us -> none  [local(): jnp.einsum('rm,sm->rs', picked, standard, preferred_element_type=jnp.floa...]
    lt x1 -> x0, other arithmetic: 10.2 us -> none  [local(): live = within < jnp.take(panel_rows, owner_ids)]
    and x1 -> x0, other arithmetic: 9.9 us -> none  [local(): picked = jnp.take(all_rows, jnp.clip(sample_ids, 0, samples - 1), axis=0)]
    gather x1 -> x0, other arithmetic: 9.88 us -> none  [local(): picked = jnp.take(all_rows, jnp.clip(sample_ids, 0, samples - 1), axis=0)]
    convert_element_type x1 -> x0, local copies, waits for them, and re-layouts: 6.71 us -> none  [local(): jnp.repeat(present.T, local_markers // present.shape[0], axis=1)]
  transfers between devices with their start and end apart: 2 -> 0, of which waited for: 1 -> 0; matrix products, arithmetic and copies ran while one was open for 11% -> 0% of each run, Pallas kernels for 0% -> 0%
where the time goes in v1:
time: 62.1 us; the launch traced here: 61.9 us
  Pallas kernels  56.7 us (91%)
  local copies, waits for them, and re-layouts  5.15 us (8%)
    pallas_call x1, Pallas kernels, fused(): pl.pallas_call(functools.partial(kernel, mk_y, mk_z, depth * mesh.shape['...  56.7 us
    unnamed x9, local copies, waits for them, and re-layouts  5.15 us

profile of v1, /device:TPU:1, one launch (start us, length us, event | category | flops | bytes accessed | tf_op | source)
XLA Modules:
  0.0 61.9 jit_solution(1252292131077663436)
XLA Ops:
  0.0 0.0 copy-start
  0.0 1.9 %copy-done = bf16[768,2048]{1,0:T(8,128)(2,1)S(1)} copy-done((bf16[768,2048]{1,0:T(8,128)(2,1)S(1)}, bf16[768,2048]{1,0:T(8,128)(2,1)}, u32[]{:S(2)}) %copy-start) | copy-done | bytes 3145752
  1.9 0.0 copy-start.1
  1.9 0.9 %copy-done.1 = s32[32,768]{1,0:T(8,128)S(1)} copy-done((s32[32,768]{1,0:T(8,128)S(1)}, s32[32,768]{1,0:T(8,128)}, u32[]{:S(2)}) %copy-start.1) | copy-done | bytes 98328
  2.8 0.0 copy-start.2
  2.8 0.7 %copy-done.2 = f32[2048]{0:T(1024)S(1)} copy-done((f32[2048]{0:T(1024)S(1)}, f32[2048]{0:T(1024)}, u32[]{:S(2)}) %copy-start.2) | copy-done | bytes 8216
  3.5 0.0 copy-start.3
  3.5 0.7 %copy-done.3 = s32[16]{0:T(128)S(1)} copy-done((s32[16]{0:T(128)S(1)}, s32[16]{0:T(128)}, u32[]{:S(2)}) %copy-start.3) | copy-done | bytes 88
  4.1 56.7 %shard_map.46 = f32[192,1536]{1,0:T(8,128)S(1)} custom-call(bf16[768,2048]{1,0:T(8,128)(2,1)S(1)} %copy-done, f32[1,2048]{1,0:T(1,128)S(1)} %bitcast.1, s32[32,768]{1,0:T(8,128)S(1)} %copy-done.1, s32[16]{0:T(128)S(1)} %copy-done.3), custom_call_target="tpu_custom_call" | custom-call | tf_op jit(solution)/shard_map/pallas_call | solution.py:244
  60.9 1.0 %copy.6 = f32[192,1536]{1,0:T(8,128)} copy(f32[192,1536]{1,0:T(8,128)S(1)} %shard_map.46) | data formatting | bytes 2359296
Async XLA Ops:
  0.0 1.9 %copy-start = (bf16[768,2048]{1,0:T(8,128)(2,1)S(1)}, bf16[768,2048]{1,0:T(8,128)(2,1)}, u32[]{:S(2)}) copy-start(bf16[768,2048]{1,0:T(8,128)(2,1)} %dosage.1) | copy-start | bytes 9437188
  1.9 0.9 %copy-start.1 = (s32[32,768]{1,0:T(8,128)S(1)}, s32[32,768]{1,0:T(8,128)}, u32[]{:S(2)}) copy-start(s32[32,768]{1,0:T(8,128)} %present.1) | copy-start | bytes 294916
  2.8 0.7 %copy-start.2 = (f32[2048]{0:T(1024)S(1)}, f32[2048]{0:T(1024)}, u32[]{:S(2)}) copy-start(f32[2048]{0:T(1024)} %param.5) | copy-start | bytes 24580
  3.5 0.7 %copy-start.3 = (s32[16]{0:T(128)S(1)}, s32[16]{0:T(128)}, u32[]{:S(2)}) copy-start(s32[16]{0:T(128)} %rows_ref.1) | copy-start | bytes 196

commit v2 on v1

--- a/solution.py
+++ b/solution.py
@@ -23,41 +23,54 @@
     return jnp.where(v == 0.0, 0.0, jnp.where(v < 0.0, -root, root))
 
 
-def kernel(mk_y, mk_z, markers, dosage, freq, present, rows_ref, out, *scratch):
+Y_FIRST, Z_FIRST = (0, 1, 2), (1, 0, 2)
+ORDERS = [Y_FIRST] * 6
+
+
+def kernel(markers, dosage, freq_hbm, present_hbm, rows_hbm, out, *scratch):
     half, depth = dosage.shape
     row_blk = half // 3
-    hy = row_blk // mk_y
-    sl = hy // mk_z
+    size = [row_blk // 2, row_blk // 4, row_blk // 8]
+    hy = size[0]
     widths = [row_blk * (a + 1) for a in range(3)] + [half // 2] * 3
     chunks = len(widths)
     it = iter(scratch)
-    dos, std, hot = next(it), next(it), next(it)
-    ys, yr, zs, zr, acc, fin = ([next(it) for _ in range(chunks)] for _ in range(6))
-    (dos_sem, std_s, std_r, y_s, y_r, z_s, z_r, gz_s, gz_r, gy_s, gy_r, t_s, t_r) = it
+    dos, std, hot, freq, present, rows_ref = (next(it) for _ in range(6))
+    out_buf = [[next(it) for _ in range(chunks)] for _ in range(3)]
+    in_buf = [[next(it) for _ in range(chunks)] for _ in range(3)]
+    acc, fin = ([next(it) for _ in range(chunks)] for _ in range(2))
+    (load_sem, std_s, std_r, red_s, red_r, gat_s, gat_r, t_s, t_r) = it
 
     mk, t = lax.axis_index("mk"), lax.axis_index("tile")
-    y, z = lax.rem(mk, mk_y), mk // mk_y
-    oy, ot = 1 - y, 1 - t
+    y, z = lax.rem(mk, 2), mk // 2
+    low, high = lax.rem(z, 2), z // 2
+    bits = [y, low, high]
+    partners = [{"mk": mk + 1 - 2 * y}, {"mk": mk + 2 - 4 * low}, {"mk": mk + 4 - 8 * high}]
+    ot = 1 - t
+    to_t = {"tile": ot}
 
     loads = [
+        pltpu.make_async_copy(present_hbm, present, load_sem.at[3]),
+        pltpu.make_async_copy(freq_hbm, freq, load_sem.at[4]),
+        pltpu.make_async_copy(rows_hbm, rows_ref, load_sem.at[5]),
+    ]
+    for load in loads:
+        load.start()
+    dos_loads = [
         pltpu.make_async_copy(
-            dosage.at[pl.ds(a * row_blk, row_blk)], dos.at[pl.ds(a * row_blk, row_blk)], dos_sem.at[a]
+            dosage.at[pl.ds(a * row_blk, row_blk)], dos.at[pl.ds(a * row_blk, row_blk)], load_sem.at[a]
         )
         for a in range(3)
     ]
-    for load in loads:
+    for load in dos_loads:
         load.start()
 
-    to_y = {"mk": z * mk_y + oy}
-    to_t = {"tile": ot}
-
-    def to_z(k):
-        return {"mk": lax.rem(z + k, mk_z) * mk_y + y}
-
     barrier = pltpu.get_barrier_semaphore()
-    peers = [to_y, to_t] + [to_z(k) for k in range(1, mk_z)]
+    peers = partners + [to_t]
     for peer in peers:
         pl.semaphore_signal(barrier, inc=1, device_id=peer, device_id_type=MESH)
+    for load in loads:
+        load.wait()
 
     owner = mk * 2 + t
     start = jnp.int32(0)
@@ -120,34 +133,33 @@
         view = std.at[pl.ds(pl.multiple_of(core * half + a * row_blk, 128), row_blk)]
         return remote(view, view, std_s.at[a], std_r.at[a], to_t)
 
-    def y_copy(c):
-        return remote(ys[c], yr[c], y_s.at[c], y_r.at[c], to_y)
-
-    def zrows(r):
-        return pl.ds(pl.multiple_of(r * sl, sl), sl)
-
-    def z_copy(c, k, source):
-        return remote(zs[c].at[zrows(lax.rem(z + k, mk_z))], zr[c].at[zrows(source)], z_s.at[c, k], z_r.at[c, k], to_z(k))
-
-    def gz_copy(c, k, source):
-        view = fin[c].at[t, pl.ds(pl.multiple_of(y * hy + source * sl, sl), sl)]
-        return remote(view, view, gz_s.at[c, k], gz_r.at[c, k], to_z(k))
-
-    def gy_copy(c, which):
-        view = fin[c].at[t, pl.ds(pl.multiple_of(which * hy, hy), hy)]
-        return remote(view, view, gy_s.at[c], gy_r.at[c], to_y)
+    def base(c, level):
+        row = 0
+        for l in range(level):
+            row = row + bits[ORDERS[c][l]] * size[l]
+        return row
+
+    def red_copy(c, l):
+        return remote(out_buf[l][c], in_buf[l][c], red_s.at[c, l], red_r.at[c, l], partners[ORDERS[c][l]])
+
+    def gat_copy(c, l, mine):
+        bit = bits[ORDERS[c][l]]
+        row = base(c, l) + (bit if mine else 1 - bit) * size[l]
+        view = fin[c].at[t, pl.ds(pl.multiple_of(row, size[l]), size[l])]
+        return remote(view, view, gat_s.at[c, l], gat_r.at[c, l], partners[ORDERS[c][l]])
 
     def t_copy(c, step, core):
-        which = y if step == 0 else oy
+        bit = bits[ORDERS[c][0]]
+        which = bit if step == 0 else 1 - bit
         view = fin[c].at[core, pl.ds(pl.multiple_of(which * hy, hy), hy)]
         return remote(view, view, t_s.at[c, step], t_r.at[c, step], to_t)
 
     def send_half(c):
-        ys[c][...] = encode(product(c, oy))
-        go(y_copy(c))
+        out_buf[0][c][...] = encode(product(c, 1 - bits[ORDERS[c][0]]))
+        go(red_copy(c, 0))
 
     def own_half(c):
-        acc[c][...] = product(c, y)
+        acc[c][...] = product(c, bits[ORDERS[c][0]])
 
     def select(c, core):
         i0, j0 = place(c, core)
@@ -164,7 +176,7 @@
             )
 
     for a in range(3):
-        loads[a].wait()
+        dos_loads[a].wait()
         standardize(a)
         if a == 0:
             pl.semaphore_wait(barrier, len(peers))
@@ -179,41 +191,46 @@
     for a in range(3, 6):
         own_half(a)
 
-    def stage_b(c):
-        y_copy(c).wait_recv()
-        total = acc[c][...] + decode(yr[c][...])
-        acc[c][...] = total
-        zs[c][...] = encode(total)
-        for k in range(1, mk_z):
-            go(z_copy(c, k, z))
-
-    def stage_c(c):
-        total = acc[c][zrows(z), :]
-        for k in range(1, mk_z):
-            source = lax.rem(z + mk_z - k, mk_z)
-            z_copy(c, k, source).wait_recv()
-            total = total + decode(zr[c][zrows(source), :])
-        fin[c][t, pl.ds(pl.multiple_of(y * hy + z * sl, sl), sl), :] = encode(total)
-        for k in range(1, mk_z):
-            go(gz_copy(c, k, z))
-
-    def stage_d(c):
-        for k in range(1, mk_z):
-            gz_copy(c, k, lax.rem(z + mk_z - k, mk_z)).wait_recv()
-        go(gy_copy(c, y))
+    def halve(c, l):
+        red_copy(c, l - 1).wait_recv()
+        rows = pl.ds(0, size[l - 1])
+        acc[c][rows, :] = acc[c][rows, :] + decode(in_buf[l - 1][c][...])
+        bit = bits[ORDERS[c][l]]
+        other = pl.ds(pl.multiple_of((1 - bit) * size[l], size[l]), size[l])
+        mine = pl.ds(pl.multiple_of(bit * size[l], size[l]), size[l])
+        out_buf[l][c][...] = encode(acc[c][other, :])
+        go(red_copy(c, l))
+        acc[c][pl.ds(0, size[l]), :] = acc[c][mine, :]
+
+    def finish(c):
+        red_copy(c, 2).wait_recv()
+        total = acc[c][pl.ds(0, size[2]), :] + decode(in_buf[2][c][...])
+        fin[c][t, pl.ds(pl.multiple_of(base(c, 3), size[2]), size[2]), :] = encode(total)
+        go(gat_copy(c, 2, True))
+
+    def gather_1(c):
+        gat_copy(c, 2, False).wait_recv()
+        go(gat_copy(c, 1, True))
+
+    def gather_2(c):
+        gat_copy(c, 1, False).wait_recv()
+        go(gat_copy(c, 0, True))
         go(t_copy(c, 0, t))
 
-    def stage_e(c):
-        gy_copy(c, oy).wait_recv()
+    def gather_3(c):
+        gat_copy(c, 0, False).wait_recv()
         go(t_copy(c, 1, t))
         select(c, t)
 
-    def stage_f(c):
+    def others(c):
         t_copy(c, 0, ot).wait_recv()
         t_copy(c, 1, ot).wait_recv()
         select(c, ot)
 
-    stages = [stage_b, stage_c, stage_d, stage_e, stage_f]
+    stages = [
+        functools.partial(halve, l=1), functools.partial(halve, l=2),
+        finish, gather_1, gather_2, gather_3, others,
+    ]
     for s in range(chunks + len(stages) - 1):
         for d, stage in enumerate(stages):
             if 0 <= s - d < chunks:
@@ -225,27 +242,30 @@
 
 
 def fused(mesh, dosage, allele_freq, present, panel_rows):
-    mk_y, mk_z = 2, mesh.shape["mk"] // 2
     half, depth = dosage.shape
     samples = 2 * half
     panel_max = 2 * samples // (2 * mesh.shape["mk"])
     row_blk = half // 3
     widths = [row_blk * (a + 1) for a in range(3)] + [half // 2] * 3
-    hy = row_blk // 2
     bf, f32 = jnp.bfloat16, jnp.float32
-    scratch = [pltpu.VMEM((half, depth), bf), pltpu.VMEM((samples, depth), bf), pltpu.VMEM((panel_max, samples), bf)]
-    for dtype in (bf, bf, bf, bf, f32):
-        scratch += [pltpu.VMEM((hy, w), dtype) for w in widths]
+    scratch = [
+        pltpu.VMEM((half, depth), bf), pltpu.VMEM((samples, depth), bf), pltpu.VMEM((panel_max, samples), bf),
+        pltpu.VMEM((1, depth), f32), pltpu.VMEM(present.shape, present.dtype),
+        pltpu.SMEM(panel_rows.shape, panel_rows.dtype),
+    ]
+    for _ in range(2):
+        for parts in (2, 4, 8):
+            scratch += [pltpu.VMEM((row_blk // parts, w), bf) for w in widths]
+    scratch += [pltpu.VMEM((row_blk // 2, w), f32) for w in widths]
     scratch += [pltpu.VMEM((2, row_blk, w), bf) for w in widths]
     n = len(widths)
-    for shape in [(3,)] * 3 + [(n,)] * 2 + [(n, mk_z)] * 4 + [(n,)] * 2 + [(n, 2)] * 2:
+    for shape in [(6,)] + [(3,)] * 2 + [(n, 3)] * 4 + [(n, 2)] * 2:
         scratch.append(pltpu.SemaphoreType.DMA(shape))
-    vmem = pl.BlockSpec(memory_space=pltpu.VMEM)
     return pl.pallas_call(
-        functools.partial(kernel, mk_y, mk_z, depth * mesh.shape["mk"]),
+        functools.partial(kernel, depth * mesh.shape["mk"]),
         out_shape=jax.ShapeDtypeStruct((panel_max, samples), f32),
-        in_specs=[pl.BlockSpec(memory_space=pl.ANY), vmem, vmem, pl.BlockSpec(memory_space=pltpu.SMEM)],
-        out_specs=vmem,
+        in_specs=[pl.BlockSpec(memory_space=pltpu.HBM)] * 4,
+        out_specs=pl.BlockSpec(memory_space=pltpu.VMEM),
         scratch_shapes=scratch,
         compiler_params=pltpu.CompilerParams(
             collective_id=0, has_side_effects=True, vmem_limit_bytes=44 * 1024 * 1024

time: 62.1 us -> 56.7 us (0.913)
  Pallas kernels: 56.7 us -> 51.4 us
    pallas_call x1, Pallas kernels: 56.7 us -> 51.4 us  [fused(): pl.pallas_call(functools.partial(kernel, depth * mesh.shape['mk']), out_s...]
where the time goes in v2:
time: 56.7 us; the launch traced here: 56.5 us
  Pallas kernels  51.4 us (91%)
  local copies, waits for them, and re-layouts  5.15 us (9%)
    pallas_call x1, Pallas kernels, fused(): pl.pallas_call(functools.partial(kernel, depth * mesh.shape['mk']), out_s...  51.4 us
    unnamed x9, local copies, waits for them, and re-layouts  5.15 us

profile of v2, /device:TPU:1, one launch (start us, length us, event | category | flops | bytes accessed | tf_op | source)
XLA Modules:
  0.0 56.5 jit_solution(11737520825683249591)
XLA Ops:
  0.0 0.0 copy-start
  0.0 1.9 %copy-done = bf16[768,2048]{1,0:T(8,128)(2,1)S(1)} copy-done((bf16[768,2048]{1,0:T(8,128)(2,1)S(1)}, bf16[768,2048]{1,0:T(8,128)(2,1)}, u32[]{:S(2)}) %copy-start) | copy-done | bytes 3145752
  1.9 0.0 copy-start.1
  1.9 0.9 %copy-done.1 = s32[32,768]{1,0:T(8,128)S(1)} copy-done((s32[32,768]{1,0:T(8,128)S(1)}, s32[32,768]{1,0:T(8,128)}, u32[]{:S(2)}) %copy-start.1) | copy-done | bytes 98328
  2.8 0.0 copy-start.2
  2.8 0.7 %copy-done.2 = f32[2048]{0:T(1024)S(1)} copy-done((f32[2048]{0:T(1024)S(1)}, f32[2048]{0:T(1024)}, u32[]{:S(2)}) %copy-start.2) | copy-done | bytes 8216
  3.5 0.0 copy-start.3
  3.5 0.7 %copy-done.3 = s32[16]{0:T(128)S(1)} copy-done((s32[16]{0:T(128)S(1)}, s32[16]{0:T(128)}, u32[]{:S(2)}) %copy-start.3) | copy-done | bytes 88
  4.1 51.4 %shard_map.46 = f32[192,1536]{1,0:T(8,128)S(1)} custom-call(bf16[768,2048]{1,0:T(8,128)(2,1)S(1)} %copy-done, f32[1,2048]{1,0:T(1,128)S(1)} %bitcast.1, s32[32,768]{1,0:T(8,128)S(1)} %copy-done.1, s32[16]{0:T(128)S(1)} %copy-done.3), custom_call_target="tpu_custom_call" | custom-call | tf_op jit(solution)/shard_map/pallas_call | solution.py:264
  55.5 1.0 %copy.6 = f32[192,1536]{1,0:T(8,128)} copy(f32[192,1536]{1,0:T(8,128)S(1)} %shard_map.46) | data formatting | bytes 2359296
Async XLA Ops:
  0.0 1.9 %copy-start = (bf16[768,2048]{1,0:T(8,128)(2,1)S(1)}, bf16[768,2048]{1,0:T(8,128)(2,1)}, u32[]{:S(2)}) copy-start(bf16[768,2048]{1,0:T(8,128)(2,1)} %dosage.1) | copy-start | bytes 9437188
  1.9 0.9 %copy-start.1 = (s32[32,768]{1,0:T(8,128)S(1)}, s32[32,768]{1,0:T(8,128)}, u32[]{:S(2)}) copy-start(s32[32,768]{1,0:T(8,128)} %present_hbm.1) | copy-start | bytes 294916
  2.8 0.7 %copy-start.2 = (f32[2048]{0:T(1024)S(1)}, f32[2048]{0:T(1024)}, u32[]{:S(2)}) copy-start(f32[2048]{0:T(1024)} %param.5) | copy-start | bytes 24580
  3.5 0.7 %copy-start.3 = (s32[16]{0:T(128)S(1)}, s32[16]{0:T(128)}, u32[]{:S(2)}) copy-start(s32[16]{0:T(128)} %rows_hbm.1) | copy-start | bytes 196

commit v3 on v2

--- a/solution.py
+++ b/solution.py
@@ -25,6 +25,7 @@
 
 Y_FIRST, Z_FIRST = (0, 1, 2), (1, 0, 2)
 ORDERS = [Y_FIRST] * 6
+AHEAD = 2
 
 
 def kernel(markers, dosage, freq_hbm, present_hbm, rows_hbm, out, *scratch):
@@ -154,9 +155,14 @@
         view = fin[c].at[core, pl.ds(pl.multiple_of(which * hy, hy), hy)]
         return remote(view, view, t_s.at[c, step], t_r.at[c, step], to_t)
 
+    first = []
+
     def send_half(c):
         out_buf[0][c][...] = encode(product(c, 1 - bits[ORDERS[c][0]]))
-        go(red_copy(c, 0))
+        if c >= AHEAD:
+            first[c - AHEAD].wait_send()
+        first.append(red_copy(c, 0))
+        first[c].start()
 
     def own_half(c):
         acc[c][...] = product(c, bits[ORDERS[c][0]])
@@ -182,15 +188,6 @@
             pl.semaphore_wait(barrier, len(peers))
         go(std_copy(a, t))
         send_half(a)
-    for a in range(3):
-        own_half(a)
-    for a in range(3):
-        std_copy(a, ot).wait_recv()
-    for a in range(3, 6):
-        send_half(a)
-    for a in range(3, 6):
-        own_half(a)
-
     def halve(c, l):
         red_copy(c, l - 1).wait_recv()
         rows = pl.ds(0, size[l - 1])
@@ -231,13 +228,21 @@
         functools.partial(halve, l=1), functools.partial(halve, l=2),
         finish, gather_1, gather_2, gather_3, others,
     ]
+    for a in range(3):
+        own_half(a)
     for s in range(chunks + len(stages) - 1):
+        if s == 1:
+            for a in range(3):
+                std_copy(a, ot).wait_recv()
+        if 1 <= s <= 3:
+            send_half(s + 2)
+            own_half(s + 2)
         for d, stage in enumerate(stages):
             if 0 <= s - d < chunks:
                 stage(s - d)
     for r in range(0, out.shape[0], 32):
         out[r : r + 32, :] = decode(out[r : r + 32, :]) * (1.0 / (markers * UP * UP))
-    for copy in sent:
+    for copy in sent + first[chunks - AHEAD :]:
         copy.wait_send()
 
 

time: 56.7 us -> 55.1 us (0.972)
  Pallas kernels: 51.4 us -> 49.7 us
    pallas_call x1, Pallas kernels: 51.4 us -> 49.7 us  [fused(): pl.pallas_call(functools.partial(kernel, depth * mesh.shape['mk']), out_s...]
where the time goes in v3:
time: 55.1 us; the launch traced here: 54.8 us
  Pallas kernels  49.7 us (90%)
  local copies, waits for them, and re-layouts  5.15 us (9%)
    pallas_call x1, Pallas kernels, fused(): pl.pallas_call(functools.partial(kernel, depth * mesh.shape['mk']), out_s...  49.7 us
    unnamed x9, local copies, waits for them, and re-layouts  5.15 us

profile of v3, /device:TPU:1, one launch (start us, length us, event | category | flops | bytes accessed | tf_op | source)
XLA Modules:
  0.0 54.8 jit_solution(14243842006508090465)
XLA Ops:
  0.0 0.0 copy-start
  0.0 1.9 %copy-done = bf16[768,2048]{1,0:T(8,128)(2,1)S(1)} copy-done((bf16[768,2048]{1,0:T(8,128)(2,1)S(1)}, bf16[768,2048]{1,0:T(8,128)(2,1)}, u32[]{:S(2)}) %copy-start) | copy-done | bytes 3145752
  1.9 0.0 copy-start.1
  1.9 0.9 %copy-done.1 = s32[32,768]{1,0:T(8,128)S(1)} copy-done((s32[32,768]{1,0:T(8,128)S(1)}, s32[32,768]{1,0:T(8,128)}, u32[]{:S(2)}) %copy-start.1) | copy-done | bytes 98328
  2.8 0.0 copy-start.2
  2.8 0.7 %copy-done.2 = f32[2048]{0:T(1024)S(1)} copy-done((f32[2048]{0:T(1024)S(1)}, f32[2048]{0:T(1024)}, u32[]{:S(2)}) %copy-start.2) | copy-done | bytes 8216
  3.5 0.0 copy-start.3
  3.5 0.7 %copy-done.3 = s32[16]{0:T(128)S(1)} copy-done((s32[16]{0:T(128)S(1)}, s32[16]{0:T(128)}, u32[]{:S(2)}) %copy-start.3) | copy-done | bytes 88
  4.1 49.7 %shard_map.46 = f32[192,1536]{1,0:T(8,128)S(1)} custom-call(bf16[768,2048]{1,0:T(8,128)(2,1)S(1)} %copy-done, f32[1,2048]{1,0:T(1,128)S(1)} %bitcast.1, s32[32,768]{1,0:T(8,128)S(1)} %copy-done.1, s32[16]{0:T(128)S(1)} %copy-done.3), custom_call_target="tpu_custom_call" | custom-call | tf_op jit(solution)/shard_map/pallas_call | solution.py:269
  53.8 1.0 %copy.6 = f32[192,1536]{1,0:T(8,128)} copy(f32[192,1536]{1,0:T(8,128)S(1)} %shard_map.46) | data formatting | bytes 2359296
Async XLA Ops:
  0.0 1.9 %copy-start = (bf16[768,2048]{1,0:T(8,128)(2,1)S(1)}, bf16[768,2048]{1,0:T(8,128)(2,1)}, u32[]{:S(2)}) copy-start(bf16[768,2048]{1,0:T(8,128)(2,1)} %dosage.1) | copy-start | bytes 9437188
  1.9 0.9 %copy-start.1 = (s32[32,768]{1,0:T(8,128)S(1)}, s32[32,768]{1,0:T(8,128)}, u32[]{:S(2)}) copy-start(s32[32,768]{1,0:T(8,128)} %present_hbm.1) | copy-start | bytes 294916
  2.8 0.7 %copy-start.2 = (f32[2048]{0:T(1024)S(1)}, f32[2048]{0:T(1024)}, u32[]{:S(2)}) copy-start(f32[2048]{0:T(1024)} %param.5) | copy-start | bytes 24580
  3.5 0.7 %copy-start.3 = (s32[16]{0:T(128)S(1)}, s32[16]{0:T(128)}, u32[]{:S(2)}) copy-start(s32[16]{0:T(128)} %rows_hbm.1) | copy-start | bytes 196
